TPU v7x, 128 devices: a whole 4x4x4 slice. The times are simulated.
128 devices in a mesh: ep: 16 (over x, z), tp: 8 (over y, core).
Axes of the slice: x: 4, y: 4, z: 4, core: 2. Of those that a mesh axis runs over, the one named last changes fastest.
Arguments:
- tokens: bfloat16 [2048, 4096], P('ep', 'tp'), may hold values from -6 to 6
- out_grad: bfloat16 [2048, 4096], P('ep', 'tp'), may hold values from -6 to 6
- routes: int32 [2048, 4], P('ep'), may hold values from 0 to 15, all different within a row; in each aligned block of 128 rows (0 to 127, 128 to 255, ...) at most 64 rows name the same one
- probs: bfloat16 [2048, 4], P('ep'), may hold values from 0.019897461 to 0.59765625
- w_in: bfloat16 [16, 2, 1536, 4096], P('ep', None, 'tp'), as said below
- w_out: bfloat16 [16, 1536, 4096], P('ep', 'tp'), as said below
Outputs:
- in_grad: bfloat16 [2048, 4096], P('ep', 'tp')
- grad_in: bfloat16 [16, 2, 1536, 4096], P('ep', None, 'tp')
- grad_out: bfloat16 [16, 1536, 4096], P('ep', 'tp')
Inputs may be any that keep to these rules, and one draw needn't show every extreme that they name: `routes`: each token names 4 different copies; within the tokens of one device (aligned blocks of 128 tokens) no copy is named more than 64 times, a bound that some block reaches. `w_in`: copies c and c + 8 hold equal weights. `w_out`: copies c and c + 8 hold equal weights.
All inputs are finite; a program needn't handle non-finite values.
Results may differ from a plain program's by a relative error of at most 0.02.
Values may be sent and summed in bfloat16 or wider, within the bound.
A program may use at most 128 MiB of HBM per device.

v0:
```python
import jax
import jax.numpy as jnp
from jax import lax
from jax.sharding import PartitionSpec as P


def partner(block, axis, apart):
    count = lax.axis_size(axis)
    route = []
    for low in range(count):
        high = low | 1 << apart
        if high != low and high < count:
            route += [(low, high), (high, low)]
    return lax.ppermute(block, axis, route)


def slot_tables(block_routes, copies, cap):
    flat = block_routes.reshape(-1)
    nrows = flat.shape[0]
    before = jnp.arange(nrows, dtype=jnp.int32)
    earlier = (before[None, :] < before[:, None]) & (flat[None, :] == flat[:, None])
    ranks = jnp.sum(earlier.astype(jnp.int32), axis=1)
    slot = flat * cap + ranks
    source = (
        jnp.full((copies * cap,), nrows, jnp.int32).at[slot].set(jnp.arange(nrows, dtype=jnp.int32))
    )
    return (slot, source)


def body(tokens, out_grad, routes, probs, w_in, w_out):
    n_ep = lax.axis_size("ep")
    tok_dev, top = routes.shape
    nrows = tok_dev * top
    cap = 2 * nrows // n_ep
    slot, source = slot_tables(routes, n_ep, cap)
    valid = source < nrows
    local = jnp.minimum(source, nrows - 1)
    tok_index = local // top
    scale = jnp.where(valid, probs.reshape(-1)[local].astype(jnp.float32), 0.0)[:, None]
    packed_x = jnp.where(valid[:, None], tokens[tok_index], jnp.zeros((), jnp.bfloat16))
    packed_g = (scale * out_grad[tok_index].astype(jnp.float32)).astype(jnp.bfloat16)
    part = tokens.shape[1]
    send_x = packed_x.reshape(n_ep, cap, part)
    send_g = packed_g.reshape(n_ep, cap, part)
    recv_x, recv_g = (
        lax.all_to_all(send_x, "ep", split_axis=0, concat_axis=0, tiled=True),
        lax.all_to_all(send_g, "ep", split_axis=0, concat_axis=0, tiled=True),
    )
    rows_x = lax.all_gather(recv_x.reshape(n_ep * cap, part), "tp", axis=1, tiled=True)
    rows_g = lax.all_gather(recv_g.reshape(n_ep * cap, part), "tp", axis=1, tiled=True)
    width = rows_x.shape[1]
    w_gate = w_in[0, 0]
    w_up = w_in[0, 1]
    w_down = w_out[0]
    contract_last = (((1,), (1,)), ((), ()))
    a = lax.dot_general(rows_x, w_gate, contract_last, preferred_element_type=jnp.float32)
    b = lax.dot_general(rows_x, w_up, contract_last, preferred_element_type=jnp.float32)
    sig = jax.nn.sigmoid(a)
    silu = a * sig
    hidden = (silu * b).astype(jnp.bfloat16)
    dh = lax.dot_general(rows_g, w_down, contract_last, preferred_element_type=jnp.float32)
    da = (dh * b * sig * (1.0 + a * (1.0 - sig))).astype(jnp.bfloat16)
    db = (dh * silu).astype(jnp.bfloat16)
    partial_rows = jnp.dot(da, w_gate, preferred_element_type=jnp.float32)
    partial_rows = partial_rows + jnp.dot(db, w_up, preferred_element_type=jnp.float32)
    summed = lax.psum_scatter(
        partial_rows.reshape(n_ep, cap, width).astype(jnp.bfloat16),
        "tp",
        scatter_dimension=2,
        tiled=True,
    )
    back = lax.all_to_all(summed, "ep", split_axis=0, concat_axis=0, tiled=True)
    picked = back.reshape(n_ep * cap, back.shape[2])[slot]
    in_grad = jnp.sum(
        picked.astype(jnp.float32).reshape(tok_dev, top, back.shape[2]), axis=1
    ).astype(jnp.bfloat16)
    contract_rows = (((0,), (0,)), ((), ()))
    own_in = jnp.stack(
        [
            lax.dot_general(da, rows_x, contract_rows, preferred_element_type=jnp.float32),
            lax.dot_general(db, rows_x, contract_rows, preferred_element_type=jnp.float32),
        ]
    ).astype(jnp.bfloat16)[None]
    own_out = lax.dot_general(
        hidden, rows_g, contract_rows, preferred_element_type=jnp.float32
    ).astype(jnp.bfloat16)[None]
    half_bit = n_ep.bit_length() - 2
    other_in, other_out = partner((own_in, own_out), "ep", half_bit)
    grad_in = (own_in.astype(jnp.float32) + other_in.astype(jnp.float32)).astype(jnp.bfloat16)
    grad_out = (own_out.astype(jnp.float32) + other_out.astype(jnp.float32)).astype(jnp.bfloat16)
    return (in_grad, grad_in, grad_out)


def solution(mesh):
    return jax.shard_map(
        body,
        mesh=mesh,
        in_specs=(
            P("ep", "tp"),
            P("ep", "tp"),
            P("ep", None),
            P("ep", None),
            P("ep", None, "tp", None),
            P("ep", "tp", None),
        ),
        out_specs=(P("ep", "tp"), P("ep", None, "tp", None), P("ep", "tp", None)),
        check_vma=False,
    )
```

profile of v0, /device:TPU:0, one launch (start us, length us, event | category | flops | bytes accessed | tf_op | source)
XLA Modules:
  0.0 329.8 jit_solution(15195773333764695855)
XLA Ops:
  7.2 0.0 copy-start
  7.2 0.0 all-gather.5.cloned.1.call-start
  7.2 0.8 broadcast_multiply_fusion
  8.0 0.8 copy.13
  8.8 0.8 copy.14
  9.6 0.1 reshape.126
  9.8 0.1 copy.12
  9.9 0.1 mul.50
  10.0 0.1 eq.15
  10.1 0.3 convert_reduce_fusion
  10.4 2.4 scatter_custom_fusion
  12.9 6.8 %gather_fusion = bf16[1024]{0:T(1024)(128)(2,1)S(1)} fusion(bf16[512]{0:T(512)(128)(2,1)S(1)} %reshape.126, s32[1024]{0:T(1024)S(1)} %get-tuple-element.7), kind=kCustom, calls=%fused_computation | custom fusion | bytes 8192 | tf_op jit(solution)/shard_map/gather | solution.py:39
  19.7 0.1 broadcast_in_dim.36
  19.8 4.0 %gather_fusion.2 = bf16[1024,512]{1,0:T(8,128)(2,1)S(1)} fusion(bf16[128,512]{1,0:T(8,128)(2,1)S(1)} %copy-done.2, s32[1024]{0:T(1024)S(1)} %get-tuple-element.8), kind=kCustom, calls=%fused_computation.2 | custom fusion | bytes 2101248 | tf_op jit(solution)/shard_map/gather | solution.py:40
  23.7 0.0 copy-start.3
  23.7 0.2 broadcast_select_fusion
  24.0 24.7 %all_to_all.15 = bf16[16,64,512]{2,1,0:T(8,128)(2,1)} all-to-all(bf16[16,64,512]{2,1,0:T(8,128)(2,1)S(1)} %broadcast_select_fusion), channel_id=1, replica_groups=mesh['ep'=16,'tp'=8] {'ep'}, dimensions={0} | all-to-all | bytes 2097152 | tf_op jit(solution)/shard_map/all_to_all | solution.py:46
  48.7 0.0 all-gather.5.cloned.1.call-update
  48.7 0.0 all-gather.3.cloned.1.call-start
  48.7 0.1 mul.51
  48.8 4.0 %gather_fusion.1 = bf16[1024,512]{1,0:T(8,128)(2,1)S(1)} fusion(bf16[128,512]{1,0:T(8,128)(2,1)S(1)} %copy-done.3, s32[1024]{0:T(1024)S(1)} %get-tuple-element.8), kind=kCustom, calls=%fused_computation.1 | custom fusion | bytes 2101248 | tf_op jit(solution)/shard_map/gather | solution.py:41
  52.8 0.3 fusion.3
  53.1 19.7 %all_to_all.16 = bf16[16,64,512]{2,1,0:T(8,128)(2,1)} all-to-all(bf16[16,64,512]{2,1,0:T(8,128)(2,1)S(1)} %fusion.3), channel_id=1, replica_groups=mesh['ep'=16,'tp'=8] {'ep'}, dimensions={0} | all-to-all | bytes 2097152 | tf_op jit(solution)/shard_map/all_to_all | solution.py:47
  72.8 0.0 all-gather.3.cloned.1.call-update
  72.8 0.2 reduce-scatter.2.cloned.1.call-start
  73.0 23.9 %all-gather.5.cloned.1.call-done = bf16[1024,4096]{1,0:T(8,128)(2,1)} async-done(((bf16[1024,512]{1,0:T(8,128)(2,1)}), bf16[1024,4096]{1,0:T(8,128)(2,1)}) %all-gather.5.cloned.1.call-update) | async-done | bytes 8388624 | tf_op jit(solution)/shard_map/all_gather | solution.py:49
  96.9 7.7 %fusion.6 = f32[1024,192]{0,1:T(8,128)} fusion(bf16[1024,4096]{1,0:T(8,128)(2,1)} %all-gather.5.cloned.1.call-done, bf16[1,2,192,4096]{3,2,1,0:T(8,128)(2,1)} %param.10), kind=kOutput, calls=%fused_computation.19 | convolution fusion | flops 1610612736 | bytes 10747904 | tf_op jit(solution)/shard_map/dot_general | solution.py:56
  104.6 3.8 %fusion.9 = f32[1024,192]{0,1:T(8,128)} fusion(bf16[1024,4096]{1,0:T(8,128)(2,1)S(1)} %copy-done.7, bf16[1,2,192,4096]{3,2,1,0:T(8,128)(2,1)S(1)} %copy-done.5), kind=kOutput, calls=%fused_computation.22 | convolution fusion | flops 1610612736 | bytes 10747904 | tf_op jit(solution)/shard_map/dot_general | solution.py:57
  108.4 40.1 %all-gather.3.cloned.1.call-done = bf16[1024,4096]{1,0:T(8,128)(2,1)} async-done(((bf16[1024,512]{1,0:T(8,128)(2,1)}), bf16[1024,4096]{1,0:T(8,128)(2,1)}) %all-gather.3.cloned.1.call-update) | async-done | bytes 8388624 | tf_op jit(solution)/shard_map/all_gather | solution.py:50
  148.5 6.9 %multiply_convert_fusion.1 = (bf16[1024,192]{0,1:T(8,128)(2,1)S(1)}, bf16[1024,192]{0,1:T(8,128)(2,1)S(1)}) fusion(f32[1024,192]{0,1:T(8,128)} %fusion.6, f32[1024,192]{0,1:T(8,128)} %fusion.9, bf16[1024,4096]{1,0:T(8,128)(2,1)} %all-gather.3.cloned.1.call-done, bf16[1,192,4096]{2,1,0:T(8,128)(2,1)S(1)} %copy-done), kind=kOutput, calls=%fused_computation.35 | convolution fusion | flops 1613168640 | bytes 12320768 | tf_op jit(solution)/shard_map/dot_general | solution.py:61
  155.5 8.1 %fusion.4 = f32[1024,4096]{1,0:T(8,128)} fusion(bf16[1024,192]{0,1:T(8,128)(2,1)S(1)} %get-tuple-element.6, bf16[1,2,192,4096]{3,2,1,0:T(8,128)(2,1)S(1)} %copy-done.6), kind=kOutput, calls=%fused_computation.17 | convolution fusion | flops 1610612736 | bytes 18743296 | tf_op jit(solution)/shard_map/dot_general | solution.py:64
  163.6 11.4 %add_convert_fusion = bf16[1024,4096]{1,0:T(8,128)(2,1)} fusion(f32[1024,4096]{1,0:T(8,128)} %fusion.4, bf16[1024,192]{0,1:T(8,128)(2,1)S(1)} %get-tuple-element.5, bf16[1,2,192,4096]{3,2,1,0:T(8,128)(2,1)S(1)} %copy-done.6), kind=kOutput, calls=%fused_computation.5 | convolution fusion | flops 1619001344 | bytes 27131904 | tf_op jit(solution)/shard_map/dot_general | solution.py:65
  175.1 0.0 reduce-scatter.2.cloned.1.call-update
  175.1 5.6 %fusion.1 = bf16[1,1,192,4096]{3,2,1,0:T(8,128)(2,1)S(1)} fusion(bf16[1024,192]{0,1:T(8,128)(2,1)S(1)} %get-tuple-element.5, bf16[1024,4096]{1,0:T(8,128)(2,1)} %all-gather.5.cloned.1.call-done), kind=kOutput, calls=%fused_computation.11 | convolution fusion | flops 1611399168 | bytes 10354688 | tf_op jit(solution)/shard_map/dot_general | solution.py:81
  180.7 5.4 %fusion = bf16[1,1,192,4096]{3,2,1,0:T(8,128)(2,1)S(1)} fusion(bf16[1024,192]{0,1:T(8,128)(2,1)S(1)} %get-tuple-element.6, bf16[1024,4096]{1,0:T(8,128)(2,1)} %all-gather.5.cloned.1.call-done), kind=kOutput, calls=%fused_computation.10 | convolution fusion | flops 1611399168 | bytes 10354688 | tf_op jit(solution)/shard_map/dot_general | solution.py:80
  186.1 1.9 pad_maximum_fusion
  188.1 0.3 copy-done.4
  188.4 3.0 collective-permute-start
  191.4 1.8 fusion.2
  193.2 0.6 collective-permute-start.1
  193.9 100.4 %collective-permute-done.1 = bf16[1,192,4096]{2,1,0:T(8,128)(2,1)S(1)} collective-permute-done((bf16[1,192,4096]{2,1,0:T(8,128)(2,1)S(1)}, bf16[1,192,4096]{2,1,0:T(8,128)(2,1)S(1)}, u32[]{:S(2)}, u32[]{:S(2)}) %collective-permute-start.1) | collective-permute-done | bytes 1572896 | tf_op jit(solution)/shard_map/ppermute | solution.py:14
  294.3 1.7 add_convert_fusion.2
  295.9 6.8 %all-to-all-start.2 = ((bf16[16,64,512]{2,1,0:T(8,128)(2,1)}), bf16[16,64,512]{2,1,0:T(8,128)(2,1)S(1)}, u32[]{:S(2)}, u32[]{:S(2)}) async-start(bf16[16,64,512]{2,1,0:T(8,128)(2,1)} %reduce-scatter.2.cloned.1.call-done), calls=%async_computation.3 | async-start | bytes 2097152 | tf_op jit(solution)/shard_map/all_to_all | solution.py:72
  302.7 5.3 %add_convert_fusion.1 = bf16[1,2,192,4096]{3,2,1,0:T(8,128)(2,1)} fusion(bf16[1,2,192,4096]{3,2,1,0:T(8,128)(2,1)} %collective-permute-done, bf16[1,1,192,4096]{3,2,1,0:T(8,128)(2,1)S(1)} %fusion.1, bf16[1,1,192,4096]{3,2,1,0:T(8,128)(2,1)} %copy-done.4), kind=kLoop, calls=%fused_computation.6 | loop fusion | flops 7864320 | bytes 9437184 | tf_op jit(solution)/shard_map/convert_element_type | solution.py:89
  308.1 11.8 %all-to-all-done.2 = bf16[16,64,512]{2,1,0:T(8,128)(2,1)S(1)} async-done(((bf16[16,64,512]{2,1,0:T(8,128)(2,1)}), bf16[16,64,512]{2,1,0:T(8,128)(2,1)S(1)}, u32[]{:S(2)}, u32[]{:S(2)}) %all-to-all-start.2) | async-done | bytes 1048608 | tf_op jit(solution)/shard_map/all_to_all | solution.py:72
  319.9 2.0 gather_fusion.3
  321.8 0.1 gather.21
  322.0 1.3 reduce_sum.25
  (29 shorter events, 0.1 us)
Async XLA Ops:
  7.2 141.3 %copy-start = (bf16[1,192,4096]{2,1,0:T(8,128)(2,1)S(1)}, bf16[1,192,4096]{2,1,0:T(8,128)(2,1)}, u32[]{:S(2)}) copy-start(bf16[1,192,4096]{2,1,0:T(8,128)(2,1)} %param.11) | copy-start | bytes 4718596
  7.2 12.6 %copy-start.2 = (bf16[128,512]{1,0:T(8,128)(2,1)S(1)}, bf16[128,512]{1,0:T(8,128)(2,1)}, u32[]{:S(2)}) copy-start(bf16[128,512]{1,0:T(8,128)(2,1)} %param.6) | copy-start | bytes 393220
  7.2 89.7 %all-gather.5.cloned.1.call-start = ((), (), s32[]{:S(2)}) async-start(), calls=%async_computation.5 | async-start | bytes 9437184 | tf_op jit(solution)/shard_map/all_gather | solution.py:49
  23.7 25.1 %copy-start.3 = (bf16[128,512]{1,0:T(8,128)(2,1)S(1)}, bf16[128,512]{1,0:T(8,128)(2,1)}, u32[]{:S(2)}) copy-start(bf16[128,512]{1,0:T(8,128)(2,1)} %param.7) | copy-start | bytes 393220
  48.7 99.8 %all-gather.3.cloned.1.call-start = ((), (), s32[]{:S(2)}) async-start(), calls=%async_computation.4 | async-start | bytes 9437184 | tf_op jit(solution)/shard_map/all_gather | solution.py:50
  72.8 223.2 %reduce-scatter.2.cloned.1.call-start = ((), (), s32[]{:S(2)}) async-start(), calls=%async_computation.6 | async-start | bytes 9437184 | tf_op jit(solution)/shard_map/reduce_scatter | solution.py:66
  96.9 7.7 %copy-start.5 = (bf16[1,2,192,4096]{3,2,1,0:T(8,128)(2,1)S(1)}, bf16[1,2,192,4096]{3,2,1,0:T(8,128)(2,1)}, u32[]{:S(2)}) copy-start(bf16[1,2,192,4096]{3,2,1,0:T(8,128)(2,1)} %param.10) | copy-start | bytes 9437188
  96.9 7.7 %copy-start.7 = (bf16[1024,4096]{1,0:T(8,128)(2,1)S(1)}, bf16[1024,4096]{1,0:T(8,128)(2,1)}, u32[]{:S(2)}) copy-start(bf16[1024,4096]{1,0:T(8,128)(2,1)} %all-gather.5.cloned.1.call-done) | copy-start | bytes 25165828
  148.5 7.0 %copy-start.6 = (bf16[1,2,192,4096]{3,2,1,0:T(8,128)(2,1)S(1)}, bf16[1,2,192,4096]{3,2,1,0:T(8,128)(2,1)}, u32[]{:S(2)}) copy-start(bf16[1,2,192,4096]{3,2,1,0:T(8,128)(2,1)} %param.10) | copy-start | bytes 9437188
  175.1 16.3 %slice-start = ((s8[8388608]{0:T(1024)(128)(4,1)}), s8[4194304]{0:T(1024)(128)(4,1)S(1)}, s32[]{:S(2)}) async-start(s8[8388608]{0:T(1024)(128)(4,1)} %bitcast.50), calls=%async_computation.7 | async-start | bytes 8388608
  180.7 10.7 %slice-start.1 = ((s8[8388608]{0:T(1024)(128)(4,1)}), s8[4194304]{0:T(1024)(128)(4,1)S(1)}, s32[]{:S(2)}) async-start(s8[8388608]{0:T(1024)(128)(4,1)} %bitcast.50), calls=%async_computation.8 | async-start | bytes 8388608
  186.1 2.3 copy-start.4
  186.1 5.3 %copy-start.8 = (f32[1024,192]{0,1:T(8,128)S(1)}, f32[1024,192]{0,1:T(8,128)}, u32[]{:S(2)}) copy-start(f32[1024,192]{0,1:T(8,128)} %fusion.6) | copy-start | bytes 2359300
  186.1 5.3 %copy-start.9 = (f32[1024,192]{0,1:T(8,128)S(1)}, f32[1024,192]{0,1:T(8,128)}, u32[]{:S(2)}) copy-start(f32[1024,192]{0,1:T(8,128)} %fusion.9) | copy-start | bytes 2359300
  188.4 114.4 %collective-permute-start = (bf16[1,2,192,4096]{3,2,1,0:T(8,128)(2,1)}, bf16[1,2,192,4096]{3,2,1,0:T(8,128)(2,1)}, u32[]{:S(2)}, u32[]{:S(2)}) collective-permute-start(bf16[1,2,192,4096]{3,2,1,0:T(8,128)(2,1)} %pad_maximum_fusion), channel_id=1, source_target_pairs={{0,64},{64,0},{8,72},{72,8},{16,80},{80,16},{24,88},{88,24},{32,96... | collective-permute-start | bytes 9437192 | tf_op jit(solution)/shard_map/ppermute | solution.py:14
  193.2 101.0 %collective-permute-start.1 = (bf16[1,192,4096]{2,1,0:T(8,128)(2,1)S(1)}, bf16[1,192,4096]{2,1,0:T(8,128)(2,1)S(1)}, u32[]{:S(2)}, u32[]{:S(2)}) collective-permute-start(bf16[1,192,4096]{2,1,0:T(8,128)(2,1)S(1)} %fusion.2), channel_id=1, source_target_pairs={{0,64},{64,0},{8,72},{72,8},{16,80},{80,16},{24,88},{88,24},{32,96... | collective-permute-start | bytes 4718600 | tf_op jit(solution)/shard_map/ppermute | solution.py:14
  295.9 23.9 %all-to-all-start.2 = ((bf16[16,64,512]{2,1,0:T(8,128)(2,1)}), bf16[16,64,512]{2,1,0:T(8,128)(2,1)S(1)}, u32[]{:S(2)}, u32[]{:S(2)}) async-start(bf16[16,64,512]{2,1,0:T(8,128)(2,1)} %reduce-scatter.2.cloned.1.call-done), calls=%async_computation.3 | async-start | bytes 2097152 | tf_op jit(solution)/shard_map/all_to_all | solution.py:72
  319.9 3.4 %copy-start.1 = (bf16[1,192,4096]{2,1,0:T(8,128)(2,1)S(1)}, bf16[1,192,4096]{2,1,0:T(8,128)(2,1)}, u32[]{:S(2)}) copy-start(bf16[1,192,4096]{2,1,0:T(8,128)(2,1)} %param.11) | copy-start | bytes 4718596
Sparse Core Ops, SparseCore 0:
  48.8 48.0 all-gather.4
  98.6 49.8 all-gather.2
  175.2 52.6 reduce-scatter.1
where the time goes:
time: 330 us
  waiting for transfers between devices  176 us (53%)
  matrix products  50.8 us (15%)
  blocking collectives  44.4 us (13%)
  local copies, waits for them, and re-layouts  21.8 us (7%)
  between operations  14 us (4%)
  other arithmetic  11.9 us (4%)
  starting transfers between devices  10.7 us (3%)
    ppermute x2, waiting for transfers between devices, partner(): return lax.ppermute(block, axis, route)  100 us
    all_gather x1, waiting for transfers between devices, body(): lax.all_gather(recv_g.reshape(n_ep * cap, part), 'tp', axis=1, tiled=True)  40.1 us
    all_to_all x1, blocking collectives, body(): lax.all_to_all(send_x, 'ep', split_axis=0, concat_axis=0, tiled=True)  24.7 us
    all_gather x1, waiting for transfers between devices, body(): lax.all_gather(recv_x.reshape(n_ep * cap, part), 'tp', axis=1, tiled=True)  23.9 us
    all_to_all x1, blocking collectives, body(): lax.all_to_all(send_g, 'ep', split_axis=0, concat_axis=0, tiled=True)  19.7 us
    all_to_all x1, waiting for transfers between devices, body(): back = lax.all_to_all(summed, 'ep', split_axis=0, concat_axis=0, tiled=True)  11.8 us
    dot_general x1, matrix products, body(): jnp.dot(db, w_up, preferred_element_type=jnp.float32)  11.4 us
    dot_general x1, matrix products, body(): partial_rows = jnp.dot(da, w_gate, preferred_element_type=jnp.float32)  8.15 us
  transfers between devices with their start and end apart: 6, of which 4 were waited for; matrix products, arithmetic and copies ran while one was open for 11% of the time, Pallas kernels for 0%

commit v1 on v0

--- a/solution.py
+++ b/solution.py
@@ -47,7 +47,16 @@
         lax.all_to_all(send_g, "ep", split_axis=0, concat_axis=0, tiled=True),
     )
     rows_x = lax.all_gather(recv_x.reshape(n_ep * cap, part), "tp", axis=1, tiled=True)
-    rows_g = lax.all_gather(recv_g.reshape(n_ep * cap, part), "tp", axis=1, tiled=True)
+    _mark_runs = lambda point, a_name, array_axis: jnp.concatenate(
+        lax.all_to_all(
+            jnp.stack([point for _ in range(lax.psum(1, a_name))]),
+            axis_name=a_name,
+            split_axis=0,
+            concat_axis=0,
+        ),
+        axis=array_axis,
+    )
+    rows_g = _mark_runs(recv_g.reshape(n_ep * cap, part), "tp", 1)
     width = rows_x.shape[1]
     w_gate = w_in[0, 0]
     w_up = w_in[0, 1]

time: 330 us -> 365 us (1.11)
  waiting for transfers between devices: 176 us -> 197 us
  local copies, waits for them, and re-layouts: 21.8 us -> 27.7 us
  starting transfers between devices: 10.7 us -> 15.8 us
    all_to_all x0 -> x1, waiting for transfers between devices: none -> 62.3 us  [body(): lax.all_to_all(jnp.stack([point for _ in range(lax.psum(1, a_name))]), ax...]
    all_gather x1 -> x0, waiting for transfers between devices: 40.1 us -> none  [body(): lax.all_gather(recv_g.reshape(n_ep * cap, part), 'tp', axis=1, tiled=True)]
    another operation x0 -> x2, local copies, waits for them, and re-layouts: none -> 5.79 us  [body(): jnp.stack([point for _ in range(lax.psum(1, a_name))])]
    ppermute x2, waiting for transfers between devices: 100 us -> 95.2 us  [partner(): return lax.ppermute(block, axis, route)]
    all_to_all x0 -> x1, starting transfers between devices: none -> 4.96 us  [body(): lax.all_to_all(jnp.stack([point for _ in range(lax.psum(1, a_name))]), ax...]
    dot_general x1, matrix products: 1.83 us -> 6.45 us  [body(): lax.dot_general(hidden, rows_g, contract_rows, preferred_element_type=jnp...]
    all_gather x1, waiting for transfers between devices: 23.9 us -> 27.8 us  [body(): lax.all_gather(recv_x.reshape(n_ep * cap, part), 'tp', axis=1, tiled=True)]
  transfers between devices with their start and end apart: 6 -> 6, of which waited for: 4 -> 4; matrix products, arithmetic and copies ran while one was open for 11% -> 13% of each run, Pallas kernels for 0% -> 0%
where the time goes in v1:
time: 365 us
  waiting for transfers between devices  197 us (54%)
  matrix products  54 us (15%)
  blocking collectives  44.4 us (12%)
  local copies, waits for them, and re-layouts  27.7 us (8%)
  starting transfers between devices  15.8 us (4%)
  between operations  14.3 us (4%)
  other arithmetic  11.8 us (3%)
    ppermute x2, waiting for transfers between devices, partner(): return lax.ppermute(block, axis, route)  95.2 us
    all_to_all x1, waiting for transfers between devices, body(): lax.all_to_all(jnp.stack([point for _ in range(lax.psum(1, a_name))]), ax...  62.3 us
    all_gather x1, waiting for transfers between devices, body(): lax.all_gather(recv_x.reshape(n_ep * cap, part), 'tp', axis=1, tiled=True)  27.8 us
    all_to_all x1, blocking collectives, body(): lax.all_to_all(send_x, 'ep', split_axis=0, concat_axis=0, tiled=True)  24.7 us
    all_to_all x1, blocking collectives, body(): lax.all_to_all(send_g, 'ep', split_axis=0, concat_axis=0, tiled=True)  19.7 us
    dot_general x1, matrix products, body(): jnp.dot(db, w_up, preferred_element_type=jnp.float32)  11.4 us
    all_to_all x1, waiting for transfers between devices, body(): back = lax.all_to_all(summed, 'ep', split_axis=0, concat_axis=0, tiled=True)  11.2 us
    dot_general x1, matrix products, body(): partial_rows = jnp.dot(da, w_gate, preferred_element_type=jnp.float32)  8.15 us
  transfers between devices with their start and end apart: 6, of which 4 were waited for; matrix products, arithmetic and copies ran while one was open for 13% of the time, Pallas kernels for 0%

profile of v1, /device:TPU:0, one launch (start us, length us, event | category | flops | bytes accessed | tf_op | source)
XLA Modules:
  0.0 364.5 jit_solution(12937359871356525795)
XLA Ops:
  7.2 0.0 copy-start
  7.2 0.0 all-gather.2.cloned.1.call-start
  7.2 0.9 copy.14
  8.1 0.7 broadcast_multiply_fusion
  8.8 0.1 eq.15
  8.9 0.3 convert_reduce_fusion
  9.2 0.1 copy.13
  9.3 0.1 mul.50
  9.4 2.4 scatter_custom_fusion
  11.9 0.8 copy.15
  12.7 0.1 reshape.131
  12.9 6.8 %gather_fusion = bf16[1024]{0:T(1024)(128)(2,1)S(1)} fusion(bf16[512]{0:T(512)(128)(2,1)S(1)} %reshape.131, s32[1024]{0:T(1024)S(1)} %get-tuple-element.7), kind=kCustom, calls=%fused_computation | custom fusion | bytes 8192 | tf_op jit(solution)/shard_map/gather | solution.py:39
  19.7 0.1 broadcast_in_dim.36
  19.8 4.0 %gather_fusion.2 = bf16[1024,512]{1,0:T(8,128)(2,1)S(1)} fusion(bf16[128,512]{1,0:T(8,128)(2,1)S(1)} %copy-done.2, s32[1024]{0:T(1024)S(1)} %get-tuple-element.8), kind=kCustom, calls=%fused_computation.2 | custom fusion | bytes 2101248 | tf_op jit(solution)/shard_map/gather | solution.py:40
  23.7 0.2 broadcast_select_fusion
  24.0 24.7 %all_to_all.20 = bf16[16,64,512]{2,1,0:T(8,128)(2,1)} all-to-all(bf16[16,64,512]{2,1,0:T(8,128)(2,1)S(1)} %broadcast_select_fusion), channel_id=1, replica_groups=mesh['ep'=16,'tp'=8] {'ep'}, dimensions={0} | all-to-all | bytes 2097152 | tf_op jit(solution)/shard_map/all_to_all | solution.py:46
  48.7 0.0 all-gather.2.cloned.1.call-update
  48.7 0.1 mul.51
  48.8 4.0 %gather_fusion.1 = bf16[1024,512]{1,0:T(8,128)(2,1)S(1)} fusion(bf16[128,512]{1,0:T(8,128)(2,1)S(1)} %copy-done.3, s32[1024]{0:T(1024)S(1)} %get-tuple-element.8), kind=kCustom, calls=%fused_computation.1 | custom fusion | bytes 2101248 | tf_op jit(solution)/shard_map/gather | solution.py:41
  52.7 0.3 fusion.3
  53.0 19.7 %all_to_all.21 = bf16[16,64,512]{2,1,0:T(8,128)(2,1)} all-to-all(bf16[16,64,512]{2,1,0:T(8,128)(2,1)S(1)} %fusion.3), channel_id=1, replica_groups=mesh['ep'=16,'tp'=8] {'ep'}, dimensions={0} | all-to-all | bytes 2097152 | tf_op jit(solution)/shard_map/all_to_all | solution.py:47
  72.7 1.5 copy.16
  74.2 4.3 %stack.12 = bf16[8,1024,512]{1,2,0:T(8,128)(2,1)} broadcast(bf16[1024,512]{0,1:T(8,128)(2,1)S(1)} %copy.16), dimensions={1,2} | broadcast | bytes 9437184 | tf_op jit(solution)/shard_map/stack | solution.py:52
  78.5 5.0 %all-to-all-start.1 = ((bf16[8,1024,512]{1,2,0:T(8,128)(2,1)}), bf16[8,1024,512]{1,2,0:T(8,128)(2,1)}, u32[]{:S(2)}, u32[]{:S(2)}) async-start(bf16[8,1024,512]{1,2,0:T(8,128)(2,1)} %stack.12), calls=%async_computation.1 | async-start | bytes 16777216 | tf_op jit(solution)/shard_map/all_to_all | solution.py:51
  83.5 0.2 reduce-scatter.2.cloned.1.call-start
  83.7 27.8 %all-gather.2.cloned.1.call-done = bf16[1024,4096]{1,0:T(8,128)(2,1)} async-done(((bf16[1024,512]{1,0:T(8,128)(2,1)}), bf16[1024,4096]{1,0:T(8,128)(2,1)}) %all-gather.2.cloned.1.call-update) | async-done | bytes 8388624 | tf_op jit(solution)/shard_map/all_gather | solution.py:49
  111.5 7.7 %fusion.6 = f32[1024,192]{0,1:T(8,128)} fusion(bf16[1024,4096]{1,0:T(8,128)(2,1)} %all-gather.2.cloned.1.call-done, bf16[1,2,192,4096]{3,2,1,0:T(8,128)(2,1)} %param.10), kind=kOutput, calls=%fused_computation.19 | convolution fusion | flops 1610612736 | bytes 10747904 | tf_op jit(solution)/shard_map/dot_general | solution.py:65
  119.3 3.8 %fusion.9 = f32[1024,192]{0,1:T(8,128)} fusion(bf16[1024,4096]{1,0:T(8,128)(2,1)S(1)} %copy-done.7, bf16[1,2,192,4096]{3,2,1,0:T(8,128)(2,1)S(1)} %copy-done.5), kind=kOutput, calls=%fused_computation.22 | convolution fusion | flops 1610612736 | bytes 10747904 | tf_op jit(solution)/shard_map/dot_general | solution.py:66
  123.0 62.3 %all-to-all-done.1 = bf16[8,1024,512]{1,2,0:T(8,128)(2,1)} async-done(((bf16[8,1024,512]{1,2,0:T(8,128)(2,1)}), bf16[8,1024,512]{1,2,0:T(8,128)(2,1)}, u32[]{:S(2)}, u32[]{:S(2)}) %all-to-all-start.1) | async-done | bytes 8388640 | tf_op jit(solution)/shard_map/all_to_all | solution.py:51
  185.3 5.9 %multiply_convert_fusion.1 = (bf16[1024,192]{0,1:T(8,128)(2,1)S(1)}, bf16[1024,192]{0,1:T(8,128)(2,1)S(1)}) fusion(f32[1024,192]{0,1:T(8,128)} %fusion.6, f32[1024,192]{0,1:T(8,128)} %fusion.9, bf16[1024,4096]{0,1:T(8,128)(2,1)} %bitcast.5, bf16[1,192,4096]{2,1,0:T(8,128)(2,1)S(1)} %copy-done), kind=kOutput, calls=%fused_computation.35 | convolution fusion | flops 1613168640 | bytes 12320768 | tf_op jit(solution)/shard_map/dot_general | solution.py:70
  191.2 8.2 %fusion.4 = f32[1024,4096]{1,0:T(8,128)} fusion(bf16[1024,192]{0,1:T(8,128)(2,1)S(1)} %get-tuple-element.6, bf16[1,2,192,4096]{3,2,1,0:T(8,128)(2,1)S(1)} %copy-done.6), kind=kOutput, calls=%fused_computation.17 | convolution fusion | flops 1610612736 | bytes 18743296 | tf_op jit(solution)/shard_map/dot_general | solution.py:73
  199.4 11.4 %add_convert_fusion = bf16[1024,4096]{1,0:T(8,128)(2,1)} fusion(f32[1024,4096]{1,0:T(8,128)} %fusion.4, bf16[1024,192]{0,1:T(8,128)(2,1)S(1)} %get-tuple-element.5, bf16[1,2,192,4096]{3,2,1,0:T(8,128)(2,1)S(1)} %copy-done.6), kind=kOutput, calls=%fused_computation.5 | convolution fusion | flops 1619001344 | bytes 27131904 | tf_op jit(solution)/shard_map/dot_general | solution.py:74
  210.8 0.0 reduce-scatter.2.cloned.1.call-update
  210.8 5.4 %fusion = bf16[1,1,192,4096]{3,2,1,0:T(8,128)(2,1)S(1)} fusion(bf16[1024,192]{0,1:T(8,128)(2,1)S(1)} %get-tuple-element.6, bf16[1024,4096]{1,0:T(8,128)(2,1)} %all-gather.2.cloned.1.call-done), kind=kOutput, calls=%fused_computation.10 | convolution fusion | flops 1611399168 | bytes 10354688 | tf_op jit(solution)/shard_map/dot_general | solution.py:89
  216.3 5.2 %fusion.1 = bf16[1,1,192,4096]{3,2,1,0:T(8,128)(2,1)S(1)} fusion(bf16[1024,192]{0,1:T(8,128)(2,1)S(1)} %get-tuple-element.5, bf16[1024,4096]{1,0:T(8,128)(2,1)} %all-gather.2.cloned.1.call-done), kind=kOutput, calls=%fused_computation.11 | convolution fusion | flops 1611399168 | bytes 10354688 | tf_op jit(solution)/shard_map/dot_general | solution.py:90
  221.5 1.9 pad_maximum_fusion
  223.4 0.3 copy-done.4
  223.7 3.0 collective-permute-start
  226.7 6.4 %fusion.2 = bf16[1,192,4096]{2,1,0:T(8,128)(2,1)S(1)} fusion(bf16[1024,4096]{0,1:T(8,128)(2,1)} %bitcast.5, f32[1024,192]{0,1:T(8,128)S(1)} %copy-done.9, f32[1024,192]{0,1:T(8,128)S(1)} %copy-done.8), kind=kOutput, calls=%fused_computation.12 | convolution fusion | flops 1612578816 | bytes 11534336 | tf_op jit(solution)/shard_map/dot_general | solution.py:93
  233.2 0.6 collective-permute-start.1
  233.8 95.2 %collective-permute-done.1 = bf16[1,192,4096]{2,1,0:T(8,128)(2,1)S(1)} collective-permute-done((bf16[1,192,4096]{2,1,0:T(8,128)(2,1)S(1)}, bf16[1,192,4096]{2,1,0:T(8,128)(2,1)S(1)}, u32[]{:S(2)}, u32[]{:S(2)}) %collective-permute-start.1) | collective-permute-done | bytes 1572896 | tf_op jit(solution)/shard_map/ppermute | solution.py:14
  329.1 1.7 add_convert_fusion.2
  330.8 7.0 %all-to-all-start.3 = ((bf16[16,64,512]{2,1,0:T(8,128)(2,1)}), bf16[16,64,512]{2,1,0:T(8,128)(2,1)S(1)}, u32[]{:S(2)}, u32[]{:S(2)}) async-start(bf16[16,64,512]{2,1,0:T(8,128)(2,1)} %reduce-scatter.2.cloned.1.call-done), calls=%async_computation.4 | async-start | bytes 2097152 | tf_op jit(solution)/shard_map/all_to_all | solution.py:81
  337.8 5.3 %add_convert_fusion.1 = bf16[1,2,192,4096]{3,2,1,0:T(8,128)(2,1)} fusion(bf16[1,2,192,4096]{3,2,1,0:T(8,128)(2,1)} %collective-permute-done, bf16[1,1,192,4096]{3,2,1,0:T(8,128)(2,1)} %copy-done.4, bf16[1,1,192,4096]{3,2,1,0:T(8,128)(2,1)S(1)} %fusion), kind=kLoop, calls=%fused_computation.6 | loop fusion | flops 7864320 | bytes 9437184 | tf_op jit(solution)/shard_map/convert_element_type | solution.py:98
  343.1 11.2 %all-to-all-done.3 = bf16[16,64,512]{2,1,0:T(8,128)(2,1)S(1)} async-done(((bf16[16,64,512]{2,1,0:T(8,128)(2,1)}), bf16[16,64,512]{2,1,0:T(8,128)(2,1)S(1)}, u32[]{:S(2)}, u32[]{:S(2)}) %all-to-all-start.3) | async-done | bytes 1048608 | tf_op jit(solution)/shard_map/all_to_all | solution.py:81
  354.3 2.0 gather_fusion.3
  356.2 0.1 gather.21
  356.4 1.3 reduce_sum.25
  (25 shorter events, 0.1 us)
Async XLA Ops:
  7.2 178.2 %copy-start = (bf16[1,192,4096]{2,1,0:T(8,128)(2,1)S(1)}, bf16[1,192,4096]{2,1,0:T(8,128)(2,1)}, u32[]{:S(2)}) copy-start(bf16[1,192,4096]{2,1,0:T(8,128)(2,1)} %param.11) | copy-start | bytes 4718596
  7.2 12.6 %copy-start.2 = (bf16[128,512]{1,0:T(8,128)(2,1)S(1)}, bf16[128,512]{1,0:T(8,128)(2,1)}, u32[]{:S(2)}) copy-start(bf16[128,512]{1,0:T(8,128)(2,1)} %param.6) | copy-start | bytes 393220
  7.2 104.3 %all-gather.2.cloned.1.call-start = ((), (), s32[]{:S(2)}) async-start(), calls=%async_computation.5 | async-start | bytes 9437184 | tf_op jit(solution)/shard_map/all_gather | solution.py:49
  23.7 25.0 %copy-start.3 = (bf16[128,512]{1,0:T(8,128)(2,1)S(1)}, bf16[128,512]{1,0:T(8,128)(2,1)}, u32[]{:S(2)}) copy-start(bf16[128,512]{1,0:T(8,128)(2,1)} %param.7) | copy-start | bytes 393220
  78.5 106.8 %all-to-all-start.1 = ((bf16[8,1024,512]{1,2,0:T(8,128)(2,1)}), bf16[8,1024,512]{1,2,0:T(8,128)(2,1)}, u32[]{:S(2)}, u32[]{:S(2)}) async-start(bf16[8,1024,512]{1,2,0:T(8,128)(2,1)} %stack.12), calls=%async_computation.1 | async-start | bytes 16777216 | tf_op jit(solution)/shard_map/all_to_all | solution.py:51
  83.5 247.3 %reduce-scatter.2.cloned.1.call-start = ((), (), s32[]{:S(2)}) async-start(), calls=%async_computation.6 | async-start | bytes 9437184 | tf_op jit(solution)/shard_map/reduce_scatter | solution.py:75
  111.5 7.7 %copy-start.5 = (bf16[1,2,192,4096]{3,2,1,0:T(8,128)(2,1)S(1)}, bf16[1,2,192,4096]{3,2,1,0:T(8,128)(2,1)}, u32[]{:S(2)}) copy-start(bf16[1,2,192,4096]{3,2,1,0:T(8,128)(2,1)} %param.10) | copy-start | bytes 9437188
  111.5 7.7 %copy-start.7 = (bf16[1024,4096]{1,0:T(8,128)(2,1)S(1)}, bf16[1024,4096]{1,0:T(8,128)(2,1)}, u32[]{:S(2)}) copy-start(bf16[1024,4096]{1,0:T(8,128)(2,1)} %all-gather.2.cloned.1.call-done) | copy-start | bytes 25165828
  185.3 5.9 %copy-start.6 = (bf16[1,2,192,4096]{3,2,1,0:T(8,128)(2,1)S(1)}, bf16[1,2,192,4096]{3,2,1,0:T(8,128)(2,1)}, u32[]{:S(2)}) copy-start(bf16[1,2,192,4096]{3,2,1,0:T(8,128)(2,1)} %param.10) | copy-start | bytes 9437188
  221.5 2.3 copy-start.4
  221.5 5.2 %copy-start.8 = (f32[1024,192]{0,1:T(8,128)S(1)}, f32[1024,192]{0,1:T(8,128)}, u32[]{:S(2)}) copy-start(f32[1024,192]{0,1:T(8,128)} %fusion.6) | copy-start | bytes 2359300
  221.5 5.2 %copy-start.9 = (f32[1024,192]{0,1:T(8,128)S(1)}, f32[1024,192]{0,1:T(8,128)}, u32[]{:S(2)}) copy-start(f32[1024,192]{0,1:T(8,128)} %fusion.9) | copy-start | bytes 2359300
  223.7 114.0 %collective-permute-start = (bf16[1,2,192,4096]{3,2,1,0:T(8,128)(2,1)}, bf16[1,2,192,4096]{3,2,1,0:T(8,128)(2,1)}, u32[]{:S(2)}, u32[]{:S(2)}) collective-permute-start(bf16[1,2,192,4096]{3,2,1,0:T(8,128)(2,1)} %pad_maximum_fusion), channel_id=1, source_target_pairs={{0,64},{64,0},{8,72},{72,8},{16,80},{80,16},{24,88},{88,24},{32,96... | collective-permute-start | bytes 9437192 | tf_op jit(solution)/shard_map/ppermute | solution.py:14
  233.2 95.9 %collective-permute-start.1 = (bf16[1,192,4096]{2,1,0:T(8,128)(2,1)S(1)}, bf16[1,192,4096]{2,1,0:T(8,128)(2,1)S(1)}, u32[]{:S(2)}, u32[]{:S(2)}) collective-permute-start(bf16[1,192,4096]{2,1,0:T(8,128)(2,1)S(1)} %fusion.2), channel_id=1, source_target_pairs={{0,64},{64,0},{8,72},{72,8},{16,80},{80,16},{24,88},{88,24},{32,96... | collective-permute-start | bytes 4718600 | tf_op jit(solution)/shard_map/ppermute | solution.py:14
  330.8 23.5 %all-to-all-start.3 = ((bf16[16,64,512]{2,1,0:T(8,128)(2,1)}), bf16[16,64,512]{2,1,0:T(8,128)(2,1)S(1)}, u32[]{:S(2)}, u32[]{:S(2)}) async-start(bf16[16,64,512]{2,1,0:T(8,128)(2,1)} %reduce-scatter.2.cloned.1.call-done), calls=%async_computation.4 | async-start | bytes 2097152 | tf_op jit(solution)/shard_map/all_to_all | solution.py:81
  354.3 3.4 copy-start.1
Sparse Core Ops, SparseCore 0:
  48.8 62.6 all-gather.1
  210.9 52.4 reduce-scatter.1
